TPU v7x, 32 devices: a whole 2x2x4 slice. The times are simulated.
32 devices in a mesh: shards: 4 (over y, x), tensor: 4 (over z), section: 2 (over core).
Axes of the slice: x: 2, y: 2, z: 4, core: 2. Of those that a mesh axis runs over, the one named last changes fastest.
Arguments:
- gradient: bfloat16 [4, 768, 2048], P('section', 'tensor', 'shards'), may hold values from -36 to 36, as said below
- weight: bfloat16 [4, 768, 2048], P('section', 'tensor', 'shards'), may hold values from -0.21875 to 0.21875
- projector: float32 [4, 768, 256], P('section', 'tensor'), may hold values from -0.21875 to 0.21875
- first_moment: float32 [4, 256, 2048], P('section', 'tensor', 'shards'), may hold values from -0.3125 to 0.3125
- squared_moment: float32 [4, 256, 2048], P('section', 'tensor', 'shards'), may hold values from 1e-07 to 1e-05
- step_count: int32 [4], P('section'), may hold values from 1 to 11
- norm_gains: float32 [4, 768], P('section', 'tensor'), may hold values from 0.5 to 1.5
- gain_gradient: float32 [4, 768], P('section', 'tensor'), may hold values from -0.15625 to 0.15625
- gain_first: float32 [4, 768], P('section', 'tensor'), may hold values from -0.046875 to 0.046875
- gain_second: float32 [4, 768], P('section', 'tensor'), may hold values from 1e-08 to 1e-06
Outputs:
- weight_next: bfloat16 [4, 768, 2048], P('section', 'tensor', 'shards')
- fresh_projector: float32 [4, 768, 256], P('section', 'tensor')
- new_first: float32 [4, 256, 2048], P('section', 'tensor', 'shards')
- new_second: float32 [4, 256, 2048], P('section', 'tensor', 'shards')
- new_gains: float32 [4, 768], P('section', 'tensor')
- new_gain_first: float32 [4, 768], P('section', 'tensor')
- new_gain_second: float32 [4, 768], P('section', 'tensor')
Inputs may be any that keep to these rules, and one draw needn't show every extreme that they name: `gradient`: gradient entries are finite real numbers.
All inputs are finite; a program needn't handle non-finite values.
Results may differ from a plain program's by a relative error of at most 0.001.
Values sent between devices are 32-bit elements; how exact they have to be, the bound alone decides.
A program may use at most 64 MiB of HBM per device.

v0:
```python
import jax
import jax.numpy as jnp
from jax import lax
from jax.sharding import PartitionSpec as P

NS_STEPS = 5


BETA_ONE = 0.9
BETA_TWO = 0.999
EPSILON = 1e-08
NORM_EPS = 1e-06
LEARN_RATE = 0.01
GALORE_SCALE = 0.25
WEIGHT_DECAY = 0.1


def polynomial_steps(current, gram_matrix):
    precision_highest = lax.Precision.HIGHEST
    identity = jnp.eye(gram_matrix.shape[1], dtype=jnp.float32)[None]
    series_coefficients = jnp.broadcast_to(identity, gram_matrix.shape)
    for sweep_index in range(NS_STEPS):
        factor = 1.5 * identity - 0.5 * gram_matrix
        series_coefficients = jnp.einsum(
            "mrs,mst->mrt", series_coefficients, factor, precision=precision_highest
        )
        if sweep_index + 1 < NS_STEPS:
            inner = jnp.einsum("mrs,mst->mrt", factor, gram_matrix, precision=precision_highest)
            gram_matrix = jnp.einsum("mrs,mst->mrt", inner, factor, precision=precision_highest)
    return jnp.einsum("mdr,mrs->mds", current, series_coefficients, precision=precision_highest)


def spread_orthogonalize(ranged):
    precision_highest = lax.Precision.HIGHEST
    squares = lax.psum(jnp.sum(ranged * ranged, axis=(1, 2)), ("shards", "tensor"))
    current = ranged / (jnp.sqrt(squares) + NORM_EPS)[:, None, None]
    gram_matrix = lax.psum(
        jnp.einsum("mdr,mds->mrs", current, current, precision=precision_highest),
        ("shards", "tensor"),
    )
    return polynomial_steps(current, gram_matrix)


def shards(
    gradient,
    weight,
    projector,
    first_moment,
    squared_moment,
    step_count,
    norm_gains,
    gain_gradient,
    gain_first,
    gain_second,
):
    precision_highest = lax.Precision.HIGHEST
    gradient_widened = gradient.astype(jnp.float32)
    folded = lax.psum(
        jnp.einsum("mdf,mdr->mfr", gradient_widened, projector, precision=precision_highest),
        "tensor",
    )
    ranged_part = jnp.einsum("mdf,mfr->mdr", gradient_widened, folded, precision=precision_highest)
    ranged = lax.psum_scatter(ranged_part, "shards", scatter_dimension=1, tiled=True)
    fresh_projector = lax.all_gather(spread_orthogonalize(ranged), "shards", axis=1, tiled=True)
    projected_slice = jnp.einsum(
        "uqk,uqc->ukc", fresh_projector, gradient_widened, precision=precision_highest
    )
    own_rank = first_moment.shape[1]
    complete_rows = lax.psum(projected_slice, "tensor")
    projected = lax.dynamic_slice_in_dim(
        complete_rows, lax.axis_index("tensor") * own_rank, own_rank, 1
    )
    steps_float = step_count.astype(jnp.float32)[:, None, None]
    new_first = BETA_ONE * first_moment + (1.0 - BETA_ONE) * projected
    new_second = BETA_TWO * squared_moment + (1.0 - BETA_TWO) * projected * projected
    direction = (
        new_first
        / (1.0 - BETA_ONE**steps_float)
        / (jnp.sqrt(new_second / (1.0 - BETA_TWO**steps_float)) + EPSILON)
    )
    update = jnp.einsum(
        "hxp,hpq->hxq",
        fresh_projector,
        lax.all_gather(direction, "tensor", axis=1, tiled=True),
        precision=precision_highest,
    )
    weight_float = weight.astype(jnp.float32)
    weight_next = (
        weight_float - LEARN_RATE * (GALORE_SCALE * update + WEIGHT_DECAY * weight_float)
    ).astype(jnp.bfloat16)
    gain_steps = step_count.astype(jnp.float32)[:, None]
    new_gain_first = BETA_ONE * gain_first + (1.0 - BETA_ONE) * gain_gradient
    new_gain_second = BETA_TWO * gain_second + (1.0 - BETA_TWO) * gain_gradient * gain_gradient
    new_gains = norm_gains - LEARN_RATE * (new_gain_first / (1.0 - BETA_ONE**gain_steps)) / (
        jnp.sqrt(new_gain_second / (1.0 - BETA_TWO**gain_steps)) + EPSILON
    )
    return (
        weight_next,
        fresh_projector,
        new_first,
        new_second,
        new_gains,
        new_gain_first,
        new_gain_second,
    )


def solution(mesh):
    return jax.shard_map(
        shards,
        mesh=mesh,
        in_specs=(
            P("section", "tensor", "shards"),
            P("section", "tensor", "shards"),
            P("section", "tensor", None),
            P("section", "tensor", "shards"),
            P("section", "tensor", "shards"),
            P("section"),
            P("section", "tensor"),
            P("section", "tensor"),
            P("section", "tensor"),
            P("section", "tensor"),
        ),
        out_specs=(
            P("section", "tensor", "shards"),
            P("section", "tensor", None),
            P("section", "tensor", "shards"),
            P("section", "tensor", "shards"),
            P("section", "tensor"),
            P("section", "tensor"),
            P("section", "tensor"),
        ),
        check_vma=False,
    )
```

profile of v0, /device:TPU:0, one launch (start us, length us, event | category | flops | bytes accessed | tf_op | source)
XLA Modules:
  0.0 354.6 jit_solution(10973249222897305256)
XLA Ops:
  7.2 0.9 copy-done
  8.2 2.7 fusion.61
  10.9 54.6 %all-reduce.4.cloned.1.call-done = f32[2,512,256]{2,1,0:T(8,128)} async-done(((f32[2,512,256]{2,1,0:T(8,128)}), f32[2,512,256]{2,1,0:T(8,128)}) %all-reduce.4.cloned.1.call-update) | async-done | bytes 1048592 | tf_op jit(solution)/shard_map/psum | solution.py:58
  65.6 2.6 convolution_bitcast_fusion
  68.2 24.8 %reduce-scatter.2.cloned.1.call-done = f32[2,48,256]{2,1,0:T(8,128)} async-done(((f32[2,192,256]{2,1,0:T(8,128)}), f32[2,48,256]{2,1,0:T(8,128)}) %reduce-scatter.2.cloned.1.call-update) | async-done | bytes 98320 | tf_op jit(solution)/shard_map/reduce_scatter | solution.py:63
  93.0 1.1 multiply_reduce_fusion
  94.1 40.9 %psum.29 = f32[2]{0:T(128)S(1)} all-reduce(f32[2]{0:T(128)S(1)} %multiply_reduce_fusion), channel_id=1, replica_groups=mesh['shards'=4,'tensor'=4,'section'=2] {'shards','tensor'}, use_global_device_ids=true, to_apply=%region_3.0 | all-reduce | flops 2 | bytes 16 | tf_op jit(solution)/shard_map/psum | solution.py:35
  135.0 1.5 fusion.45
  136.6 105.6 %all-reduce.6.cloned.1.call-done = f32[2,256,256]{2,1,0:T(8,128)} async-done(((f32[2,256,256]{2,1,0:T(8,128)}), f32[2,256,256]{2,1,0:T(8,128)}) %all-reduce.6.cloned.1.call-update) | async-done | bytes 524304 | tf_op jit(solution)/shard_map/psum | solution.py:37
  242.2 1.9 fusion.14
  244.2 0.7 fusion.13
  244.8 0.7 fusion.11
  245.5 0.6 fusion.15
  246.2 0.7 fusion.12
  246.9 0.7 fusion.10
  247.6 0.7 fusion.8
  248.3 0.7 fusion.9
  249.0 0.7 fusion.7
  249.7 0.7 fusion.5
  250.4 0.7 fusion.6
  251.1 0.7 fusion.4
  251.8 0.7 fusion.62
  252.9 9.8 %all_gather.6 = f32[2,192,256]{2,1,0:T(8,128)S(1)} all-gather(f32[2,48,256]{2,1,0:T(8,128)S(1)} %fusion.44), channel_id=1, replica_groups=mesh['shards'=4,'tensor'=4,'section'=2] {'shards'}, dimensions={1}, use_global_device_ids=true | all-gather | bytes 491520 | tf_op jit(solution)/shard_map/all_gather | solution.py:64
  262.7 1.7 fusion.63
  264.5 0.7 copy-done.10
  265.2 49.8 %all-reduce.8.cloned.1.call-done = f32[2,256,512]{2,1,0:T(8,128)} async-done(((f32[2,256,512]{2,1,0:T(8,128)}), f32[2,256,512]{2,1,0:T(8,128)}) %all-reduce.8.cloned.1.call-update) | async-done | bytes 1048592 | tf_op jit(solution)/shard_map/psum | solution.py:69
  314.9 2.0 multiply_divide_fusion
  316.9 0.6 copy-done.6
  317.6 0.7 divide_subtract_fusion
  318.3 26.1 %all-gather.2.cloned.1.call-done = f32[2,256,512]{2,1,0:T(8,128)} async-done(((f32[2,64,512]{2,1,0:T(8,128)}), f32[2,256,512]{2,1,0:T(8,128)}) %all-gather.2.cloned.1.call-update) | async-done | bytes 1048592 | tf_op jit(solution)/shard_map/all_gather | solution.py:84
  344.4 2.9 fusion.3
  347.3 0.7 copy.21
  (34 shorter events, 0.9 us)
Async XLA Ops:
  7.2 1.0 copy-start
  7.2 58.4 %all-reduce.4.cloned.1.call-start = ((), (), s32[]{:S(2)}) async-start(), calls=%async_computation.1 | async-start | bytes 2097152 | tf_op jit(solution)/shard_map/psum | solution.py:58
  10.9 82.1 %reduce-scatter.2.cloned.1.call-start = ((), (), s32[]{:S(2)}) async-start(), calls=%async_computation.2 | async-start | bytes 491520 | tf_op jit(solution)/shard_map/reduce_scatter | solution.py:63
  68.2 174.0 %all-reduce.6.cloned.1.call-start = ((), (), s32[]{:S(2)}) async-start(), calls=%async_computation.3 | async-start | bytes 1048576 | tf_op jit(solution)/shard_map/psum | solution.py:37
  93.0 42.0 %copy-start.2 = (f32[2,48,256]{2,1,0:T(8,128)S(1)}, f32[2,48,256]{2,1,0:T(8,128)}, u32[]{:S(2)}) copy-start(f32[2,48,256]{2,1,0:T(8,128)} %reduce-scatter.2.cloned.1.call-done) | copy-start | bytes 294916
  136.5 178.4 %all-reduce.8.cloned.1.call-start = ((), (), s32[]{:S(2)}) async-start(), calls=%async_computation.4 | async-start | bytes 2097152 | tf_op jit(solution)/shard_map/psum | solution.py:69
  242.2 2.0 copy-start.1
  264.4 50.6 %copy-start.4 = (f32[2,64,512]{2,1,0:T(8,128)S(1)}, f32[2,64,512]{2,1,0:T(8,128)}, u32[]{:S(2)}) copy-start(f32[2,64,512]{2,1,0:T(8,128)} %param.14) | copy-start | bytes 786436
  264.4 50.6 %copy-start.5 = (f32[2,64,512]{2,1,0:T(8,128)S(1)}, f32[2,64,512]{2,1,0:T(8,128)}, u32[]{:S(2)}) copy-start(f32[2,64,512]{2,1,0:T(8,128)} %param.13) | copy-start | bytes 786436
  264.4 80.0 %all-gather.2.cloned.1.call-start = ((), (), s32[]{:S(2)}) async-start(), calls=%async_computation.5 | async-start | bytes 1310720 | tf_op jit(solution)/shard_map/all_gather | solution.py:84
  264.4 0.7 copy-start.10
  314.9 29.5 %copy-start.3 = (bf16[2,192,512]{2,1,0:T(8,128)(2,1)S(1)}, bf16[2,192,512]{2,1,0:T(8,128)(2,1)}, u32[]{:S(2)}) copy-start(bf16[2,192,512]{2,1,0:T(8,128)(2,1)} %param.11) | copy-start | bytes 1179652
  316.9 0.7 copy-start.6
  316.9 0.7 copy-start.7
  316.9 0.7 copy-start.8
  316.9 0.7 copy-start.9
Sparse Core Ops, SparseCore 0:
  11.0 54.5 all-reduce.3
  69.2 23.7 reduce-scatter.1
  136.6 105.5 all-reduce.5
  264.5 50.3 all-reduce.7
  317.1 27.3 all-gather.1
where the time goes:
time: 355 us
  waiting for transfers between devices  261 us (74%)
  blocking collectives  50.7 us (14%)
  matrix products  21.9 us (6%)
  between operations  14 us (4%)
  other arithmetic  3.77 us (1%)
    psum x1, waiting for transfers between devices, spread_orthogonalize(): lax.psum(jnp.einsum('mdr,mds->mrs', current, current, precision=precision...  106 us
    psum x1, waiting for transfers between devices, shards(): lax.psum(jnp.einsum('mdf,mdr->mfr', gradient_widened, projector, precisio...  54.6 us
    psum x1, waiting for transfers between devices, shards(): complete_rows = lax.psum(projected_slice, 'tensor')  49.8 us
    psum x1, blocking collectives, spread_orthogonalize(): lax.psum(jnp.sum(ranged * ranged, axis=(1, 2)), ('shards', 'tensor'))  40.9 us
    all_gather x1, waiting for transfers between devices, shards(): lax.all_gather(direction, 'tensor', axis=1, tiled=True)  26.1 us
    reduce_scatter x1, waiting for transfers between devices, shards(): lax.psum_scatter(ranged_part, 'shards', scatter_dimension=1, tiled=True)  24.8 us
    all_gather x1, blocking collectives, shards(): lax.all_gather(spread_orthogonalize(ranged), 'shards', axis=1, tiled=True)  9.82 us
  transfers between devices with their start and end apart: 5, of which 5 were waited for; matrix products, arithmetic and copies ran while one was open for 0% of the time, Pallas kernels for 0%

commit v1 on v0

v1 whole, which is shorter than its diff:
```python
import functools
import math
import jax
import jax.numpy as jnp
from jax import lax
from jax.experimental import pallas as pl
from jax.experimental.pallas import tpu as pltpu
from jax.sharding import PartitionSpec as P

NS_STEPS = 5
BETA_ONE = 0.9
BETA_TWO = 0.999
EPSILON = 1e-08
NORM_EPS = 1e-06
LEARN_RATE = 0.01
GALORE_SCALE = 0.25
WEIGHT_DECAY = 0.1

MESH = pl.DeviceIdType.MESH
NN = (((1,), (0,)), ((), ()))
TN = (((0,), (0,)), ((), ()))
NT = (((1,), (1,)), ((), ()))


def split(value):
    high = value.astype(jnp.bfloat16)
    low = (value - high.astype(jnp.float32)).astype(jnp.bfloat16)
    return high, low


def dot(left, right, dims):
    return lax.dot_general(left, right, dims, preferred_element_type=jnp.float32)


def dot_two(left, right, dims):
    return dot(left[0], right, dims) + dot(left[1], right, dims)


def dot_three(left, right, dims):
    return dot(left[0], right[0], dims) + (
        dot(left[0], right[1], dims) + dot(left[1], right[0], dims)
    )


def bit_of(index, bit):
    return lax.rem(lax.div(index, 2**bit), 2)


def across(index, bit):
    return index + 2**bit - 2 * 2**bit * bit_of(index, bit)


def halving(total, order):
    sizes, size = [], total
    for _ in order:
        size = size // 2 if size % 16 == 0 else size
        sizes.append(size)
    return sizes


def kernel(
    n_shards,
    n_tensor,
    g_ref,
    w_ref,
    p_ref,
    m_ref,
    v_ref,
    step_ref,
    ng_ref,
    gg_ref,
    gf_ref,
    gs_ref,
    wo_ref,
    po_ref,
    mo_ref,
    vo_ref,
    ngo_ref,
    gfo_ref,
    gso_ref,
    fold_part,
    fold_in,
    fold_all,
    range_part,
    range_in,
    range_all,
    gram_part,
    gram_in,
    gram_all,
    proj_part,
    proj_in,
    dir_all,
    send_sem,
    recv_sem,
):
    mats = g_ref.shape[0]
    rank = p_ref.shape[2]
    width = g_ref.shape[1]
    shard = lax.axis_index("shards")
    tensor = lax.axis_index("tensor")
    shard_bits = int(math.log2(n_shards))
    low, high = bit_of(tensor, 0), bit_of(tensor, 1)
    near = {"tensor": across(tensor, 0)}
    far = {"tensor": across(tensor, 1)}
    shard_peers = [{"shards": across(shard, bit)} for bit in range(shard_bits)]

    barrier = pltpu.get_barrier_semaphore()
    peers = [near, far] + shard_peers
    for peer in peers:
        pl.semaphore_signal(barrier, inc=1, device_id=peer, device_id_type=MESH)

    counter = [0]
    sent = []

    def send(src, dst, peer, arriving=None):
        slot = counter[0]
        counter[0] += 1

        def describe(where):
            return pltpu.make_async_remote_copy(
                src_ref=src,
                dst_ref=where,
                send_sem=send_sem.at[slot],
                recv_sem=recv_sem.at[slot],
                device_id=peer,
                device_id_type=MESH,
            )

        copy = describe(dst)
        copy.start()
        sent.append(copy)
        return describe(dst if arriving is None else arriving).wait_recv

    def scatter(part, landing):
        first = send(part.at[1 - high, 1 - low], landing.at[0], near)
        second = send(part.at[high, 1 - low], landing.at[1], near)
        yield
        first()
        part[1 - high, low] = part[1 - high, low] + landing[0]
        third = send(part.at[1 - high, low], landing.at[2], far)
        yield
        second()
        third()
        return part[high, low] + landing[1] + landing[2]

    def gather(whole):
        own = whole.at[high, low]
        from_far = send(own, own, far, whole.at[1 - high, low])
        from_near = send(own, own, near, whole.at[high, 1 - low])
        yield
        from_far()
        other = whole.at[1 - high, low]
        last = send(other, other, near, whole.at[1 - high, 1 - low])
        yield
        from_near()
        last()

    def store_ranks(part, value):
        rows = rank // n_tensor
        for one in range(2):
            for two in range(2):
                start = (2 * one + two) * rows
                part[one, two] = value[start : start + rows]

    def rows_at(ref, start, size):
        return ref.at[pl.ds(pl.multiple_of(start, 8), size)]

    def kept_start(total, order):
        start, size, places = 0, total, []
        for bit, kept in zip(order, halving(total, order)):
            places.append(start)
            if kept != size:
                start = start + bit_of(shard, bit) * kept
            size = kept
        return start, size, places

    def gather_rows(whole, total, order):
        start, size, places = kept_start(total, order)
        sizes = [total] + halving(total, order)
        for level in range(len(order) - 1, -1, -1):
            bit = order[level]
            if sizes[level] == sizes[level + 1]:
                continue
            kept = sizes[level + 1]
            own = places[level] + bit_of(shard, bit) * kept
            theirs = places[level] + (1 - bit_of(shard, bit)) * kept
            source = rows_at(whole, own, kept)
            wait = send(source, source, shard_peers[bit], rows_at(whole, theirs, kept))
            yield
            wait()

    def matrix(m):
        order = list(range(shard_bits))
        if m % 2:
            order = order[::-1]
        gradient = g_ref[m]
        store_ranks(fold_part.at[m], dot_two(split(p_ref[m]), gradient, TN))
        if m == 0:
            pl.semaphore_wait(barrier, len(peers))
        fold_all[m, high, low] = yield from scatter(fold_part.at[m], fold_in.at[m])
        yield from gather(fold_all.at[m])
        folded = fold_all[m].reshape(rank, -1)
        high_part, low_part = split(folded)
        part = range_part.at[m]
        part[...] = dot(gradient, high_part, NT) + dot(gradient, low_part, NT)
        start, size = 0, width
        used = 0
        for bit, kept in zip(order, halving(width, order)):
            mine = bit_of(shard, bit)
            landing = range_in.at[m, pl.ds(used, kept)]
            if kept != size:
                wait = send(
                    rows_at(part, start + (1 - mine) * kept, kept), landing, shard_peers[bit]
                )
                start = start + mine * kept
            else:
                wait = send(rows_at(part, start, kept), landing, shard_peers[bit])
            yield
            wait()
            if kept == size:
                sent.pop().wait_send()
            here = rows_at(part, start, kept)
            here[...] = here[...] + landing[...]
            used += kept
            size = kept
        rows_at(range_all.at[m], start, size)[...] = rows_at(part, start, size)[...]
        yield from gather_rows(range_all.at[m], width, order)
        ranged = range_all[m]
        ranged_split = split(ranged)
        gram_part[m, 0] = dot_three(ranged_split, ranged_split, TN)
        chunk_start, chunk, _ = kept_start(rank, order)
        source = rows_at(gram_part.at[m, 0], chunk_start, chunk)
        wait = send(source, gram_in.at[m, 0], near)
        yield
        wait()
        summed = gram_part.at[m, 1, pl.ds(0, chunk)]
        summed[...] = source[...] + gram_in[m, 0]
        wait = send(summed, gram_in.at[m, 1], far)
        yield
        wait()
        rows_at(gram_all.at[m], chunk_start, chunk)[...] = summed[...] + gram_in[m, 1]
        yield from gather_rows(gram_all.at[m], rank, order)
        gram = gram_all[m]
        row = lax.broadcasted_iota(jnp.int32, (rank, rank), 0)
        column = lax.broadcasted_iota(jnp.int32, (rank, rank), 1)
        diagonal = row == column
        squares = jnp.sum(
            jnp.sum(jnp.where(diagonal, gram, 0.0), axis=1, keepdims=True), axis=0, keepdims=True
        )
        scale = 1.0 / (jnp.sqrt(squares) + NORM_EPS)
        gram = gram * scale * scale
        series = None
        for sweep in range(NS_STEPS):
            factor = jnp.where(diagonal, 1.5, 0.0) - 0.5 * gram
            factor_split = split(factor)
            if series is None:
                series = factor
            else:
                series = dot_three(split(series), factor_split, NN)
            if sweep + 1 < NS_STEPS:
                inner = dot_three(factor_split, split(gram), NN)
                gram = dot_three(split(inner), factor_split, NN)
            yield
        fresh = dot_three(split(ranged * scale), split(series), NN)
        po_ref[m] = fresh
        fresh_split = split(fresh)
        store_ranks(proj_part.at[m], dot_two(fresh_split, gradient, TN))
        projected = yield from scatter(proj_part.at[m], proj_in.at[m])
        steps = jnp.full((1, 1), step_ref[m], jnp.int32).astype(jnp.float32)
        one = 1.0 - jnp.exp(steps * math.log(BETA_ONE))
        two = 1.0 - jnp.exp(steps * math.log(BETA_TWO))
        new_first = BETA_ONE * m_ref[m] + (1.0 - BETA_ONE) * projected
        new_second = BETA_TWO * v_ref[m] + (1.0 - BETA_TWO) * projected * projected
        dir_all[m, high, low] = new_first / one / (jnp.sqrt(new_second / two) + EPSILON)
        mo_ref[m] = new_first
        vo_ref[m] = new_second
        gathering = gather(dir_all.at[m])
        next(gathering)
        gain_first = BETA_ONE * gf_ref[m : m + 1] + (1.0 - BETA_ONE) * gg_ref[m : m + 1]
        gain_second = (
            BETA_TWO * gs_ref[m : m + 1]
            + (1.0 - BETA_TWO) * gg_ref[m : m + 1] * gg_ref[m : m + 1]
        )
        gfo_ref[m : m + 1] = gain_first
        gso_ref[m : m + 1] = gain_second
        ngo_ref[m : m + 1] = ng_ref[m : m + 1] - LEARN_RATE * (gain_first / one) / (
            jnp.sqrt(gain_second / two) + EPSILON
        )
        yield
        yield from gathering
        direction = dir_all[m].reshape(rank, -1)
        update = dot_three(fresh_split, split(direction), NN)
        weight = w_ref[m].astype(jnp.float32)
        wo_ref[m] = (
            weight - LEARN_RATE * (GALORE_SCALE * update + WEIGHT_DECAY * weight)
        ).astype(jnp.bfloat16)

    running = [matrix(m) for m in range(mats)]
    while running:
        for one in list(running):
            try:
                next(one)
            except StopIteration:
                running.remove(one)
    for copy in sent:
        copy.wait_send()


def count_sends(mats, width, rank, shard_bits):
    order = range(shard_bits)
    sizes = [rank] + halving(rank, order)
    cuts = sum(a != b for a, b in zip(sizes, sizes[1:]))
    sizes = [width] + halving(width, order)
    cuts += sum(a != b for a, b in zip(sizes, sizes[1:]))
    return mats * (12 + shard_bits + cuts + 2)


def shards(n_shards, n_tensor, *arguments):
    gradient, weight, projector, first, second = arguments[:5]
    mats, width, units = gradient.shape
    rank = projector.shape[2]
    rows = first.shape[1]
    shard_bits = int(math.log2(n_shards))
    chunk = ([rank] + halving(rank, range(shard_bits)))[-1]
    landing = sum(halving(width, range(shard_bits)))
    sends = count_sends(mats, width, rank, shard_bits)
    f32 = jnp.float32
    vmem = pl.BlockSpec(memory_space=pltpu.VMEM)
    smem = pl.BlockSpec(memory_space=pltpu.SMEM)
    like = [weight, projector, first, second] + list(arguments[6:7]) + list(arguments[8:10])
    return pl.pallas_call(
        functools.partial(kernel, n_shards, n_tensor),
        out_shape=[jax.ShapeDtypeStruct(a.shape, a.dtype) for a in like],
        in_specs=[vmem] * 5 + [smem] + [vmem] * 4,
        out_specs=[vmem] * 7,
        scratch_shapes=[
            pltpu.VMEM((mats, 2, 2, rows, units), f32),
            pltpu.VMEM((mats, 3, rows, units), f32),
            pltpu.VMEM((mats, 2, 2, rows, units), f32),
            pltpu.VMEM((mats, width, rank), f32),
            pltpu.VMEM((mats, landing, rank), f32),
            pltpu.VMEM((mats, width, rank), f32),
            pltpu.VMEM((mats, 2, rank, rank), f32),
            pltpu.VMEM((mats, 2, chunk, rank), f32),
            pltpu.VMEM((mats, rank, rank), f32),
            pltpu.VMEM((mats, 2, 2, rows, units), f32),
            pltpu.VMEM((mats, 3, rows, units), f32),
            pltpu.VMEM((mats, 2, 2, rows, units), f32),
            pltpu.SemaphoreType.DMA((sends,)),
            pltpu.SemaphoreType.DMA((sends,)),
        ],
        compiler_params=pltpu.CompilerParams(
            collective_id=0, has_side_effects=True, vmem_limit_bytes=48 * 2**20
        ),
    )(*arguments)


def solution(mesh):
    matrices = P("section", "tensor", "shards")
    basis = P("section", "tensor", None)
    gains = P("section", "tensor")
    return jax.shard_map(
        functools.partial(shards, mesh.shape["shards"], mesh.shape["tensor"]),
        mesh=mesh,
        in_specs=(matrices, matrices, basis, matrices, matrices, P("section")) + (gains,) * 4,
        out_specs=(matrices, basis, matrices, matrices, gains, gains, gains),
        check_vma=False,
    )
```

time: 355 us -> 120 us (0.34)
  waiting for transfers between devices: 261 us -> 0 us
  Pallas kernels: 0 us -> 106 us
  blocking collectives: 50.7 us -> 0 us
  matrix products: 21.9 us -> 0 us
  between operations: 14 us -> 0.67 us
  local copies, waits for them, and re-layouts: 3.1 us -> 12.9 us
  other arithmetic: 3.77 us -> 0 us
    psum x3 -> x0, waiting for transfers between devices: 210 us -> none  [the longest x1 106 us: spread_orthogonalize(): lax.psum(jnp.einsum('mdr,mds->mrs', current, current, precision=precision...]
    pallas_call x0 -> x1, Pallas kernels: none -> 106 us  [shards(): pl.pallas_call(functools.partial(kernel, n_shards, n_tensor), out_shape=[...]
    psum x1 -> x0, blocking collectives: 40.9 us -> none  [spread_orthogonalize(): lax.psum(jnp.sum(ranged * ranged, axis=(1, 2)), ('shards', 'tensor'))]
    all_gather x1 -> x0, waiting for transfers between devices: 26.1 us -> none  [shards(): lax.all_gather(direction, 'tensor', axis=1, tiled=True)]
    reduce_scatter x1 -> x0, waiting for transfers between devices: 24.8 us -> none  [shards(): lax.psum_scatter(ranged_part, 'shards', scatter_dimension=1, tiled=True)]
    dot_general x19 -> x0, matrix products: 21.9 us -> none  [the longest x4 4.02 us: polynomial_steps(): jnp.einsum('mrs,mst->mrt', factor, gram_matrix, precision=precision_highest)]
    all_gather x1 -> x0, blocking collectives: 9.82 us -> none  [shards(): lax.all_gather(spread_orthogonalize(ranged), 'shards', axis=1, tiled=True)]
    unnamed x23 -> x27, local copies, waits for them, and re-layouts: 3.1 us -> 12.9 us
  transfers between devices with their start and end apart: 5 -> 0, of which waited for: 5 -> 0; matrix products, arithmetic and copies ran while one was open for 0% -> 0% of each run, Pallas kernels for 0% -> 0%
where the time goes in v1:
time: 120 us; the launch traced here: 119 us
  Pallas kernels  106 us (88%)
  local copies, waits for them, and re-layouts  12.9 us (11%)
    pallas_call x1, Pallas kernels, shards(): pl.pallas_call(functools.partial(kernel, n_shards, n_tensor), out_shape=[...  106 us
    unnamed x27, local copies, waits for them, and re-layouts  12.9 us

profile of v1, /device:TPU:0, one launch (start us, length us, event | category | flops | bytes accessed | tf_op | source)
XLA Modules:
  0.0 119.4 jit_solution(14211098189443533649)
XLA Ops:
  0.6 0.0 copy-start
  0.6 1.0 copy-done
  1.6 0.0 copy-start.1
  1.6 1.0 copy-done.1
  2.6 0.0 copy-start.2
  2.6 1.0 copy-done.2
  3.6 0.0 copy-start.3
  3.6 0.9 copy-done.3
  4.6 0.0 copy-start.4
  4.6 0.9 copy-done.4
  5.5 0.0 copy-start.5
  5.5 0.7 copy-done.5
  6.2 0.0 copy-start.6
  6.2 0.7 copy-done.6
  6.9 0.0 copy-start.7
  6.9 0.7 copy-done.7
  7.6 0.0 copy-start.8
  7.6 0.7 copy-done.8
  8.3 0.0 copy-start.9
  8.3 0.7 copy-done.9
  8.9 105.8 %shard_map.153 = (bf16[2,192,512]{2,1,0:T(8,128)(2,1)S(1)}, f32[2,192,256]{2,1,0:T(8,128)S(1)}, f32[2,64,512]{2,1,0:T(8,128)S(1)}, f32[2,64,512]{2,1,0:T(8,128)S...) custom-call(bf16[2,192,512]{2,1,0:T(8,128)(2,1)S(1)} %copy-done, ...), custom_call_target="tpu_custom_call" | custom-call | tf_op jit(solution)/shard_map/pallas_call | solution.py:331
  114.7 0.7 copy.24
  115.5 0.7 copy.25
  116.2 0.7 copy.26
  116.9 0.7 copy.27
  117.6 0.6 copy.28
  118.2 0.6 copy.29
  118.8 0.6 copy.30
Async XLA Ops:
  0.6 1.0 copy-start
  1.6 1.0 copy-start.1
  2.6 1.0 copy-start.2
  3.6 0.9 copy-start.3
  4.6 0.9 copy-start.4
  5.5 0.7 copy-start.5
  6.2 0.7 copy-start.6
  6.9 0.7 copy-start.7
  7.6 0.7 copy-start.8
  8.3 0.7 copy-start.9

commit v2 on v1

--- a/solution.py
+++ b/solution.py
@@ -16,6 +16,11 @@
 GALORE_SCALE = 0.25
 WEIGHT_DECAY = 0.1
 
+LINK_RATE = 1e5
+HOP_TIME = 1.5
+STEP_TIME = 0.7
+START_LAG = 2.0
+
 MESH = pl.DeviceIdType.MESH
 NN = (((1,), (0,)), ((), ()))
 TN = (((0,), (0,)), ((), ()))
@@ -61,16 +66,16 @@
 def kernel(
     n_shards,
     n_tensor,
-    g_ref,
-    w_ref,
-    p_ref,
-    m_ref,
-    v_ref,
+    g_hbm,
+    w_hbm,
+    p_hbm,
+    m_hbm,
+    v_hbm,
     step_ref,
-    ng_ref,
-    gg_ref,
-    gf_ref,
-    gs_ref,
+    ng_hbm,
+    gg_hbm,
+    gf_hbm,
+    gs_hbm,
     wo_ref,
     po_ref,
     mo_ref,
@@ -90,10 +95,34 @@
     proj_part,
     proj_in,
     dir_all,
+    g_ref,
+    w_ref,
+    p_ref,
+    m_ref,
+    v_ref,
+    ng_ref,
+    gg_ref,
+    gf_ref,
+    gs_ref,
+    load_sem,
     send_sem,
     recv_sem,
 ):
     mats = g_ref.shape[0]
+    loads = {}
+
+    def load(name, source, target):
+        slot = load_sem.at[len(loads)]
+        loads[name] = pltpu.make_async_copy(source, target, slot)
+        loads[name].start()
+
+    def loaded(*names):
+        for name in names:
+            loads[name].wait()
+
+    for m in range(mats):
+        load(("p", m), p_hbm.at[m], p_ref.at[m])
+        load(("g", m), g_hbm.at[m], g_ref.at[m])
     rank = p_ref.shape[2]
     width = g_ref.shape[1]
     shard = lax.axis_index("shards")
@@ -108,6 +137,16 @@
     peers = [near, far] + shard_peers
     for peer in peers:
         pl.semaphore_signal(barrier, inc=1, device_id=peer, device_id_type=MESH)
+    for m in range(mats):
+        load(("m", m), m_hbm.at[m], m_ref.at[m])
+        load(("v", m), v_hbm.at[m], v_ref.at[m])
+        load(("w", m), w_hbm.at[m], w_ref.at[m])
+    for name, source, target in zip(
+        "abcd", (ng_hbm, gg_hbm, gf_hbm, gs_hbm), (ng_ref, gg_ref, gf_ref, gs_ref)
+    ):
+        load(name, source, target)
+
+    piece = 8.0 * dir_all.shape[3] * dir_all.shape[4] / LINK_RATE
 
     counter = [0]
     sent = []
@@ -134,11 +173,11 @@
     def scatter(part, landing):
         first = send(part.at[1 - high, 1 - low], landing.at[0], near)
         second = send(part.at[high, 1 - low], landing.at[1], near)
-        yield
+        yield "tensor", 2 * piece, piece
         first()
         part[1 - high, low] = part[1 - high, low] + landing[0]
         third = send(part.at[1 - high, low], landing.at[2], far)
-        yield
+        yield "tensor", piece, piece
         second()
         third()
         return part[high, low] + landing[1] + landing[2]
@@ -147,11 +186,11 @@
         own = whole.at[high, low]
         from_far = send(own, own, far, whole.at[1 - high, low])
         from_near = send(own, own, near, whole.at[high, 1 - low])
-        yield
+        yield "tensor", 2 * piece, piece
         from_far()
         other = whole.at[1 - high, low]
         last = send(other, other, near, whole.at[1 - high, 1 - low])
-        yield
+        yield "tensor", piece, piece
         from_near()
         last()
 
@@ -186,13 +225,14 @@
             theirs = places[level] + (1 - bit_of(shard, bit)) * kept
             source = rows_at(whole, own, kept)
             wait = send(source, source, shard_peers[bit], rows_at(whole, theirs, kept))
-            yield
+            yield f"shards{bit}", 8.0 * kept * rank / LINK_RATE, 8.0 * kept * rank / LINK_RATE
             wait()
 
     def matrix(m):
         order = list(range(shard_bits))
         if m % 2:
             order = order[::-1]
+        loaded(("p", m), ("g", m))
         gradient = g_ref[m]
         store_ranks(fold_part.at[m], dot_two(split(p_ref[m]), gradient, TN))
         if m == 0:
@@ -215,7 +255,7 @@
                 start = start + mine * kept
             else:
                 wait = send(rows_at(part, start, kept), landing, shard_peers[bit])
-            yield
+            yield f"shards{bit}", 8.0 * kept * rank / LINK_RATE, 8.0 * kept * rank / LINK_RATE
             wait()
             if kept == size:
                 sent.pop().wait_send()
@@ -231,12 +271,12 @@
         chunk_start, chunk, _ = kept_start(rank, order)
         source = rows_at(gram_part.at[m, 0], chunk_start, chunk)
         wait = send(source, gram_in.at[m, 0], near)
-        yield
+        yield "tensor", 8.0 * chunk * rank / LINK_RATE, 8.0 * chunk * rank / LINK_RATE
         wait()
         summed = gram_part.at[m, 1, pl.ds(0, chunk)]
         summed[...] = source[...] + gram_in[m, 0]
         wait = send(summed, gram_in.at[m, 1], far)
-        yield
+        yield "tensor", 8.0 * chunk * rank / LINK_RATE, 8.0 * chunk * rank / LINK_RATE
         wait()
         rows_at(gram_all.at[m], chunk_start, chunk)[...] = summed[...] + gram_in[m, 1]
         yield from gather_rows(gram_all.at[m], rank, order)
@@ -260,12 +300,13 @@
             if sweep + 1 < NS_STEPS:
                 inner = dot_three(factor_split, split(gram), NN)
                 gram = dot_three(split(inner), factor_split, NN)
-            yield
+            yield None
         fresh = dot_three(split(ranged * scale), split(series), NN)
         po_ref[m] = fresh
         fresh_split = split(fresh)
         store_ranks(proj_part.at[m], dot_two(fresh_split, gradient, TN))
         projected = yield from scatter(proj_part.at[m], proj_in.at[m])
+        loaded(("m", m), ("v", m))
         steps = jnp.full((1, 1), step_ref[m], jnp.int32).astype(jnp.float32)
         one = 1.0 - jnp.exp(steps * math.log(BETA_ONE))
         two = 1.0 - jnp.exp(steps * math.log(BETA_TWO))
@@ -275,7 +316,9 @@
         mo_ref[m] = new_first
         vo_ref[m] = new_second
         gathering = gather(dir_all.at[m])
-        next(gathering)
+        estimate = next(gathering)
+        if m == 0:
+            loaded("a", "b", "c", "d")
         gain_first = BETA_ONE * gf_ref[m : m + 1] + (1.0 - BETA_ONE) * gg_ref[m : m + 1]
         gain_second = (
             BETA_TWO * gs_ref[m : m + 1]
@@ -286,22 +329,33 @@
         ngo_ref[m : m + 1] = ng_ref[m : m + 1] - LEARN_RATE * (gain_first / one) / (
             jnp.sqrt(gain_second / two) + EPSILON
         )
-        yield
+        yield estimate
         yield from gathering
         direction = dir_all[m].reshape(rank, -1)
         update = dot_three(fresh_split, split(direction), NN)
+        loaded(("w", m),)
         weight = w_ref[m].astype(jnp.float32)
         wo_ref[m] = (
             weight - LEARN_RATE * (GALORE_SCALE * update + WEIGHT_DECAY * weight)
         ).astype(jnp.bfloat16)
 
-    running = [matrix(m) for m in range(mats)]
+    running = {m: matrix(m) for m in range(mats)}
+    ready = {m: m * START_LAG * piece for m in range(mats)}
+    free, now = {}, 0.0
     while running:
-        for one in list(running):
-            try:
-                next(one)
-            except StopIteration:
-                running.remove(one)
+        m = min(running, key=lambda at: (max(ready[at], now), at))
+        now = max(now, ready[m])
+        estimate = next(running[m], "done")
+        now += STEP_TIME
+        if estimate == "done":
+            del running[m]
+        elif estimate is None:
+            ready[m] = now
+        else:
+            link, charge, wait_time = estimate
+            begin = max(free.get(link, 0.0), now)
+            free[link] = begin + charge
+            ready[m] = begin + wait_time + HOP_TIME
     for copy in sent:
         copy.wait_send()
 
@@ -327,11 +381,13 @@
     f32 = jnp.float32
     vmem = pl.BlockSpec(memory_space=pltpu.VMEM)
     smem = pl.BlockSpec(memory_space=pltpu.SMEM)
+    anywhere = pl.BlockSpec(memory_space=pl.ANY)
+    held = list(arguments[:5]) + list(arguments[6:])
     like = [weight, projector, first, second] + list(arguments[6:7]) + list(arguments[8:10])
     return pl.pallas_call(
         functools.partial(kernel, n_shards, n_tensor),
         out_shape=[jax.ShapeDtypeStruct(a.shape, a.dtype) for a in like],
-        in_specs=[vmem] * 5 + [smem] + [vmem] * 4,
+        in_specs=[anywhere] * 5 + [smem] + [anywhere] * 4,
         out_specs=[vmem] * 7,
         scratch_shapes=[
             pltpu.VMEM((mats, 2, 2, rows, units), f32),
@@ -346,11 +402,15 @@
             pltpu.VMEM((mats, 2, 2, rows, units), f32),
             pltpu.VMEM((mats, 3, rows, units), f32),
             pltpu.VMEM((mats, 2, 2, rows, units), f32),
+        ]
+        + [pltpu.VMEM(a.shape, a.dtype) for a in held]
+        + [
+            pltpu.SemaphoreType.DMA((5 * mats + 4,)),
             pltpu.SemaphoreType.DMA((sends,)),
             pltpu.SemaphoreType.DMA((sends,)),
         ],
         compiler_params=pltpu.CompilerParams(
-            collective_id=0, has_side_effects=True, vmem_limit_bytes=48 * 2**20
+            collective_id=0, has_side_effects=True, vmem_limit_bytes=56 * 2**20
         ),
     )(*arguments)
 

time: 120 us -> 115 us (0.958)
  local copies, waits for them, and re-layouts: 12.9 us -> 6.57 us
  Pallas kernels: 106 us -> 108 us
    unnamed x27 -> x19, local copies, waits for them, and re-layouts: 12.9 us -> 6.57 us
    pallas_call x1, Pallas kernels: 106 us -> 108 us  [shards(): pl.pallas_call(functools.partial(kernel, n_shards, n_tensor), out_shape=[...]
where the time goes in v2:
time: 115 us
  Pallas kernels  108 us (94%)
  local copies, waits for them, and re-layouts  6.57 us (6%)
    pallas_call x1, Pallas kernels, shards(): pl.pallas_call(functools.partial(kernel, n_shards, n_tensor), out_shape=[...  108 us
    unnamed x19, local copies, waits for them, and re-layouts  6.57 us

profile of v2, /device:TPU:0, one launch (start us, length us, event | category | flops | bytes accessed | tf_op | source)
XLA Modules:
  0.0 115.2 jit_solution(65678668701666250)
XLA Ops:
  0.6 108.0 %shard_map.153 = (bf16[2,192,512]{2,1,0:T(8,128)(2,1)}, f32[2,192,256]{2,1,0:T(8,128)}, f32[2,64,512]{2,1,0:T(8,128)}, f32[2,64,512]{2,1,0:T(8,128)}, f32[2,192]...) custom-call(bf16[2,192,512]{2,1,0:T(8,128)(2,1)} %g_hbm.1, bf16[2,192,512]{2,1,0:T(8,128)(2,1)} %w_hbm.1, ...), custom_call_target="tpu_custom_call" | custom-call | tf_op jit(solution)/shard_map/pallas_call | solution.py:387
  108.6 0.0 copy-start
  108.6 1.8 %copy.24 = bf16[2,192,512]{2,1,0:T(8,128)(2,1)} copy(bf16[2,192,512]{2,1,0:T(8,128)(2,1)} %get-tuple-element.14) | data formatting | bytes 786432
  110.4 0.0 copy-done
  110.4 0.0 copy-start.2
  110.4 0.7 copy.25
  111.2 0.3 copy-done.2
  111.5 0.0 copy-start.1
  111.5 0.7 copy.26
  112.2 0.3 copy-done.1
  112.6 0.0 copy-start.5
  112.6 0.7 copy.27
  113.3 0.0 copy-done.5
  113.3 0.0 copy-start.4
  113.3 0.6 copy.28
  113.9 0.1 copy-done.4
  113.9 0.0 copy-start.3
  113.9 0.6 copy.29
  114.5 0.1 copy-done.3
  114.6 0.6 copy.30
Async XLA Ops:
  108.6 1.8 %copy-start = (f32[2,192,256]{2,1,0:T(8,128)S(1)}, f32[2,192,256]{2,1,0:T(8,128)}, u32[]{:S(2)}) copy-start(f32[2,192,256]{2,1,0:T(8,128)} %get-tuple-element.15) | copy-start | bytes 1179652
  110.4 1.1 copy-start.2
  111.5 1.0 copy-start.1
  112.6 0.7 copy-start.5
  113.3 0.7 copy-start.4
  113.9 0.7 copy-start.3

commit v3 on v2

--- a/solution.py
+++ b/solution.py
@@ -133,8 +133,17 @@
     far = {"tensor": across(tensor, 1)}
     shard_peers = [{"shards": across(shard, bit)} for bit in range(shard_bits)]
 
+    corner = {"tensor": across(across(tensor, 0), 1)}
+    others = []
+    for mask in range(1, n_shards):
+        other = shard
+        for bit in range(shard_bits):
+            if mask >> bit & 1:
+                other = across(other, bit)
+        others.append({"shards": other})
+
     barrier = pltpu.get_barrier_semaphore()
-    peers = [near, far] + shard_peers
+    peers = [near, far, corner] + others
     for peer in peers:
         pl.semaphore_signal(barrier, inc=1, device_id=peer, device_id_type=MESH)
     for m in range(mats):
@@ -216,16 +225,21 @@
     def gather_rows(whole, total, order):
         start, size, places = kept_start(total, order)
         sizes = [total] + halving(total, order)
-        for level in range(len(order) - 1, -1, -1):
-            bit = order[level]
-            if sizes[level] == sizes[level + 1]:
-                continue
-            kept = sizes[level + 1]
-            own = places[level] + bit_of(shard, bit) * kept
-            theirs = places[level] + (1 - bit_of(shard, bit)) * kept
-            source = rows_at(whole, own, kept)
-            wait = send(source, source, shard_peers[bit], rows_at(whole, theirs, kept))
-            yield f"shards{bit}", 8.0 * kept * rank / LINK_RATE, 8.0 * kept * rank / LINK_RATE
+        cuts = [at for at in range(len(order)) if sizes[at] != sizes[at + 1]]
+        source = rows_at(whole, start, size)
+        waits = []
+        for mask in range(1, 2 ** len(cuts)):
+            chosen = [at for place, at in enumerate(cuts) if mask >> place & 1]
+            peer, theirs = shard, start
+            for at in chosen:
+                bit = order[at]
+                peer = across(peer, bit)
+                theirs = theirs + (1 - 2 * bit_of(shard, bit)) * sizes[at + 1]
+            target = rows_at(whole, theirs, size)
+            waits.append(send(source, source, {"shards": peer}, target))
+        time = 8.0 * size * rank / LINK_RATE
+        yield "shards", 2 * time, 2 * time
+        for wait in waits:
             wait()
 
     def matrix(m):
@@ -270,15 +284,16 @@
         gram_part[m, 0] = dot_three(ranged_split, ranged_split, TN)
         chunk_start, chunk, _ = kept_start(rank, order)
         source = rows_at(gram_part.at[m, 0], chunk_start, chunk)
-        wait = send(source, gram_in.at[m, 0], near)
-        yield "tensor", 8.0 * chunk * rank / LINK_RATE, 8.0 * chunk * rank / LINK_RATE
-        wait()
-        summed = gram_part.at[m, 1, pl.ds(0, chunk)]
-        summed[...] = source[...] + gram_in[m, 0]
-        wait = send(summed, gram_in.at[m, 1], far)
-        yield "tensor", 8.0 * chunk * rank / LINK_RATE, 8.0 * chunk * rank / LINK_RATE
-        wait()
-        rows_at(gram_all.at[m], chunk_start, chunk)[...] = summed[...] + gram_in[m, 1]
+        waits = [
+            send(source, gram_in.at[m, at], peer) for at, peer in enumerate((near, far, corner))
+        ]
+        time = 8.0 * chunk * rank / LINK_RATE
+        yield "tensor", 4 * time, 2 * time
+        for wait in waits:
+            wait()
+        rows_at(gram_all.at[m], chunk_start, chunk)[...] = (source[...] + gram_in[m, 0]) + (
+            gram_in[m, 1] + gram_in[m, 2]
+        )
         yield from gather_rows(gram_all.at[m], rank, order)
         gram = gram_all[m]
         row = lax.broadcasted_iota(jnp.int32, (rank, rank), 0)
@@ -361,12 +376,7 @@
 
 
 def count_sends(mats, width, rank, shard_bits):
-    order = range(shard_bits)
-    sizes = [rank] + halving(rank, order)
-    cuts = sum(a != b for a, b in zip(sizes, sizes[1:]))
-    sizes = [width] + halving(width, order)
-    cuts += sum(a != b for a, b in zip(sizes, sizes[1:]))
-    return mats * (12 + shard_bits + cuts + 2)
+    return mats * (12 + shard_bits + 2 * 2**shard_bits + 3)
 
 
 def shards(n_shards, n_tensor, *arguments):
@@ -396,8 +406,8 @@
             pltpu.VMEM((mats, width, rank), f32),
             pltpu.VMEM((mats, landing, rank), f32),
             pltpu.VMEM((mats, width, rank), f32),
-            pltpu.VMEM((mats, 2, rank, rank), f32),
-            pltpu.VMEM((mats, 2, chunk, rank), f32),
+            pltpu.VMEM((mats, 1, rank, rank), f32),
+            pltpu.VMEM((mats, 3, chunk, rank), f32),
             pltpu.VMEM((mats, rank, rank), f32),
             pltpu.VMEM((mats, 2, 2, rows, units), f32),
             pltpu.VMEM((mats, 3, rows, units), f32),

time: 115 us -> 106 us (0.922)
  Pallas kernels: 108 us -> 98.6 us
    pallas_call x1, Pallas kernels: 108 us -> 98.6 us  [shards(): pl.pallas_call(functools.partial(kernel, n_shards, n_tensor), out_shape=[...]
where the time goes in v3:
time: 106 us
  Pallas kernels  98.6 us (93%)
  local copies, waits for them, and re-layouts  6.57 us (6%)
    pallas_call x1, Pallas kernels, shards(): pl.pallas_call(functools.partial(kernel, n_shards, n_tensor), out_shape=[...  98.6 us
    unnamed x19, local copies, waits for them, and re-layouts  6.57 us

profile of v3, /device:TPU:0, one launch (start us, length us, event | category | flops | bytes accessed | tf_op | source)
XLA Modules:
  0.0 105.9 jit_solution(8196307540210177255)
XLA Ops:
  0.6 98.6 %shard_map.153 = (bf16[2,192,512]{2,1,0:T(8,128)(2,1)}, f32[2,192,256]{2,1,0:T(8,128)}, f32[2,64,512]{2,1,0:T(8,128)}, f32[2,64,512]{2,1,0:T(8,128)}, f32[2,192]...) custom-call(bf16[2,192,512]{2,1,0:T(8,128)(2,1)} %g_hbm.1, bf16[2,192,512]{2,1,0:T(8,128)(2,1)} %w_hbm.1, ...), custom_call_target="tpu_custom_call" | custom-call | tf_op jit(solution)/shard_map/pallas_call | solution.py:397
  99.3 0.0 copy-start
  99.3 1.8 %copy.24 = bf16[2,192,512]{2,1,0:T(8,128)(2,1)} copy(bf16[2,192,512]{2,1,0:T(8,128)(2,1)} %get-tuple-element.14) | data formatting | bytes 786432
  101.1 0.0 copy-done
  101.1 0.0 copy-start.2
  101.1 0.7 copy.25
  101.8 0.3 copy-done.2
  102.2 0.0 copy-start.1
  102.2 0.7 copy.26
  102.9 0.3 copy-done.1
  103.2 0.0 copy-start.5
  103.2 0.7 copy.27
  103.9 0.0 copy-done.5
  103.9 0.0 copy-start.4
  103.9 0.6 copy.28
  104.5 0.1 copy-done.4
  104.6 0.0 copy-start.3
  104.6 0.6 copy.29
  105.2 0.1 copy-done.3
  105.3 0.6 copy.30
Async XLA Ops:
  99.3 1.8 %copy-start = (f32[2,192,256]{2,1,0:T(8,128)S(1)}, f32[2,192,256]{2,1,0:T(8,128)}, u32[]{:S(2)}) copy-start(f32[2,192,256]{2,1,0:T(8,128)} %get-tuple-element.15) | copy-start | bytes 1179652
  101.1 1.1 %copy-start.2 = (f32[2,64,512]{2,1,0:T(8,128)S(1)}, f32[2,64,512]{2,1,0:T(8,128)}, u32[]{:S(2)}) copy-start(f32[2,64,512]{2,1,0:T(8,128)} %get-tuple-element.16) | copy-start | bytes 786436
  102.2 1.0 copy-start.1
  103.2 0.7 copy-start.5
  103.9 0.7 copy-start.4
  104.6 0.7 copy-start.3

commit v4 on v3

--- a/solution.py
+++ b/solution.py
@@ -195,13 +195,11 @@
         own = whole.at[high, low]
         from_far = send(own, own, far, whole.at[1 - high, low])
         from_near = send(own, own, near, whole.at[high, 1 - low])
-        yield "tensor", 2 * piece, piece
+        from_corner = send(own, own, corner, whole.at[1 - high, 1 - low])
+        yield "tensor", 4 * piece, 3 * piece
         from_far()
-        other = whole.at[1 - high, low]
-        last = send(other, other, near, whole.at[1 - high, 1 - low])
-        yield "tensor", piece, piece
         from_near()
-        last()
+        from_corner()
 
     def store_ranks(part, value):
         rows = rank // n_tensor
@@ -222,21 +220,26 @@
             size = kept
         return start, size, places
 
-    def gather_rows(whole, total, order):
-        start, size, places = kept_start(total, order)
+    def partners(total, order):
+        start, _, _ = kept_start(total, order)
         sizes = [total] + halving(total, order)
         cuts = [at for at in range(len(order)) if sizes[at] != sizes[at + 1]]
+        found = []
+        for mask in range(1, 2 ** len(cuts)):
+            peer, theirs = shard, start
+            for place, at in enumerate(cuts):
+                if mask >> place & 1:
+                    peer = across(peer, order[at])
+                    theirs = theirs + (1 - 2 * bit_of(shard, order[at])) * sizes[at + 1]
+            found.append(({"shards": peer}, theirs))
+        return found
+
+    def gather_rows(whole, total, order):
+        start, size, _ = kept_start(total, order)
         source = rows_at(whole, start, size)
         waits = []
-        for mask in range(1, 2 ** len(cuts)):
-            chosen = [at for place, at in enumerate(cuts) if mask >> place & 1]
-            peer, theirs = shard, start
-            for at in chosen:
-                bit = order[at]
-                peer = across(peer, bit)
-                theirs = theirs + (1 - 2 * bit_of(shard, bit)) * sizes[at + 1]
-            target = rows_at(whole, theirs, size)
-            waits.append(send(source, source, {"shards": peer}, target))
+        for peer, theirs in partners(total, order):
+            waits.append(send(source, source, peer, rows_at(whole, theirs, size)))
         time = 8.0 * size * rank / LINK_RATE
         yield "shards", 2 * time, 2 * time
         for wait in waits:
@@ -259,7 +262,26 @@
         part[...] = dot(gradient, high_part, NT) + dot(gradient, low_part, NT)
         start, size = 0, width
         used = 0
-        for bit, kept in zip(order, halving(width, order)):
+        steps_left = list(zip(order, halving(width, order)))
+        direct = partners(width, order)
+        if len(direct) == n_shards - 1:
+            start, size, _ = kept_start(width, order)
+            landings = [range_in.at[m, pl.ds(at * size, size)] for at in range(len(direct))]
+            waits = [
+                send(rows_at(part, theirs, size), landing, peer)
+                for (peer, theirs), landing in zip(direct, landings)
+            ]
+            time = 8.0 * size * rank / LINK_RATE
+            yield "shards", 2 * time, 2 * time
+            for wait in waits:
+                wait()
+            here = rows_at(part, start, size)
+            total = here[...]
+            for landing in landings:
+                total = total + landing[...]
+            here[...] = total
+            steps_left = []
+        for bit, kept in steps_left:
             mine = bit_of(shard, bit)
             landing = range_in.at[m, pl.ds(used, kept)]
             if kept != size:

time: 106 us -> 112 us (1.057)
  Pallas kernels: 98.6 us -> 104 us
    pallas_call x1, Pallas kernels: 98.6 us -> 104 us  [shards(): pl.pallas_call(functools.partial(kernel, n_shards, n_tensor), out_shape=[...]
where the time goes in v4:
time: 112 us
  Pallas kernels  104 us (93%)
  local copies, waits for them, and re-layouts  6.57 us (6%)
    pallas_call x1, Pallas kernels, shards(): pl.pallas_call(functools.partial(kernel, n_shards, n_tensor), out_shape=[...  104 us
    unnamed x19, local copies, waits for them, and re-layouts  6.57 us

profile of v4, /device:TPU:0, one launch (start us, length us, event | category | flops | bytes accessed | tf_op | source)
XLA Modules:
  0.0 111.6 jit_solution(3710437404679287111)
XLA Ops:
  0.6 104.3 %shard_map.153 = (bf16[2,192,512]{2,1,0:T(8,128)(2,1)}, f32[2,192,256]{2,1,0:T(8,128)}, f32[2,64,512]{2,1,0:T(8,128)}, f32[2,64,512]{2,1,0:T(8,128)}, f32[2,192]...) custom-call(bf16[2,192,512]{2,1,0:T(8,128)(2,1)} %g_hbm.1, bf16[2,192,512]{2,1,0:T(8,128)(2,1)} %w_hbm.1, ...), custom_call_target="tpu_custom_call" | custom-call | tf_op jit(solution)/shard_map/pallas_call | solution.py:419
  105.0 0.0 copy-start
  105.0 1.8 %copy.24 = bf16[2,192,512]{2,1,0:T(8,128)(2,1)} copy(bf16[2,192,512]{2,1,0:T(8,128)(2,1)} %get-tuple-element.14) | data formatting | bytes 786432
  106.8 0.0 copy-done
  106.8 0.0 copy-start.2
  106.8 0.7 copy.25
  107.6 0.3 copy-done.2
  107.9 0.0 copy-start.1
  107.9 0.7 copy.26
  108.6 0.3 copy-done.1
  108.9 0.0 copy-start.5
  109.0 0.7 copy.27
  109.7 0.0 copy-done.5
  109.7 0.0 copy-start.4
  109.7 0.6 copy.28
  110.2 0.1 copy-done.4
  110.3 0.0 copy-start.3
  110.3 0.6 copy.29
  110.9 0.1 copy-done.3
  111.0 0.6 copy.30
Async XLA Ops:
  105.0 1.8 %copy-start = (f32[2,192,256]{2,1,0:T(8,128)S(1)}, f32[2,192,256]{2,1,0:T(8,128)}, u32[]{:S(2)}) copy-start(f32[2,192,256]{2,1,0:T(8,128)} %get-tuple-element.15) | copy-start | bytes 1179652
  106.8 1.1 copy-start.2
  107.9 1.0 copy-start.1
  108.9 0.7 copy-start.5
  109.7 0.7 copy-start.4
  110.3 0.7 copy-start.3
